TPU v7x, 1024 devices: a whole 4x8x16 slice. The times are simulated.
1024 devices in a mesh: row: 32 (over y_lo, x, core), col: 32 (over y_hi, z).
Axes of the slice: x: 4, y: 8 (y_hi: 2, y_lo: 4; y = y_hi * 4 + y_lo), z: 16, core: 2. Of those that a mesh axis runs over, the one named last changes fastest.
Arguments:
- stored: bfloat16 [32, 32, 32, 128, 128], P('row', 'col'), may hold values from -3 to 3, as said below
- pair_rows: int32 [32, 32, 32, 2, 2], P('row', 'col'), may hold values from 0 to 2047, as said below
- pair_cols: int32 [32, 32, 32, 2, 2], P('row', 'col'), may hold values from 0 to 2047, as said below
- block_owner: int32 [2048], replicated, may hold values from 0 to 2047, as said below
Outputs:
- window: float32 [32, 32, 32, 128, 128], P('row', 'col')
Inputs may be any that keep to these rules, and one draw needn't show every extreme that they name: A permutation of the block indices; block g lies at grid row block_owner[g] // 64, grid column (block_owner[g] // 2) % 32, place block_owner[g] % 2. `pair_rows`: entry [r, c, y, a, b] is the block index at grid row r, grid column y, place a. `pair_cols`: entry [r, c, y, a, b] is the block index at grid row p, grid column c, place b, where p = (r + q[c] - q[y]) mod 32 for a one-to-one q from grid columns to grid rows; so the row group at (r, y) is coupled, densely, to exactly one group of each grid column, these lie in distinct grid rows, and the coupling is symmetric. `stored`: zero on every 64 x 64 block whose pair_rows exceeds its pair_cols; blocks with equal row and column index are symmetric.
All inputs are finite; a program needn't handle non-finite values.
Results may differ from a plain program's by a relative error of at most 0.0003.
Values may be sent and summed in bfloat16 or wider, within the bound.
A program may use at most 32 MiB of HBM per device.

v0:
```python
import jax
import jax.numpy as jnp
from jax import lax
from jax.sharding import PartitionSpec as P


def passed_along(value, axis, steps):
    count = lax.axis_size(axis)
    pairs = [(source, (source + steps) % count) for source in range(count)]
    return lax.ppermute(value, axis, pairs)


def block_mask(row_ids, col_ids, width):
    strict = row_ids < col_ids
    return jnp.repeat(jnp.repeat(strict, width, axis=1), width, axis=2)


def to_buckets(groups, targets, count):
    selector = (targets[None, :] == jnp.arange(count, dtype=jnp.int32)[:, None]).astype(
        groups.dtype
    )
    return jnp.einsum("xc,cab->xab", selector, groups, preferred_element_type=jnp.float32).astype(
        groups.dtype
    )


def complete_tile(values, received, partner):
    mirrored = jnp.take(received, partner, axis=0)
    return values + jnp.swapaxes(mirrored, 1, 2)


def body(stored, pair_rows, pair_cols, block_owner):
    rows_count = lax.axis_size("row")
    cols_count = lax.axis_size("col")
    column = lax.axis_index("col")
    values = stored[0, 0]
    row_ids = pair_rows[0, 0]
    col_ids = pair_cols[0, 0]
    places = row_ids.shape[-1]
    width = values.shape[-1] // places
    partner = block_owner[col_ids[:, 0, 0]] // (cols_count * places)
    outgoing = jnp.where(block_mask(row_ids, col_ids, width), values, jnp.zeros_like(values))
    arrived, arrived_rows = (
        lax.all_to_all(outgoing, "col", split_axis=0, concat_axis=0, tiled=True),
        lax.all_to_all(partner, "col", split_axis=0, concat_axis=0, tiled=True),
    )
    received = lax.all_to_all(
        to_buckets(arrived, arrived_rows, rows_count),
        "row",
        split_axis=0,
        concat_axis=0,
        tiled=True,
    )
    complete = complete_tile(values, received, partner)
    ahead_tile, ahead_partner = passed_along((complete, partner), "col", -1)
    following = (column + 1) % cols_count
    diagonal = lax.dynamic_slice_in_dim(complete, column, 1, 0)
    ahead_group = lax.dynamic_slice_in_dim(complete, following, 1, 0)
    diagonal_all, ahead_all = (
        lax.all_gather(diagonal, "row", axis=0, tiled=True),
        lax.all_gather(ahead_group, "row", axis=0, tiled=True),
    )
    diag_term = jnp.einsum(
        "yab,ybc->yac",
        complete,
        jnp.take(diagonal_all, partner, axis=0),
        preferred_element_type=jnp.float32,
    )
    ahead_term = jnp.einsum(
        "yab,ybc->yac",
        ahead_tile,
        jnp.take(ahead_all, ahead_partner, axis=0),
        preferred_element_type=jnp.float32,
    )
    return (diag_term + ahead_term)[None, None]


def solution(mesh):
    in_specs = (
        P("row", "col", None, None, None),
        P("row", "col", None, None, None),
        P("row", "col", None, None, None),
        P(),
    )
    out_specs = P("row", "col", None, None, None)
    return jax.shard_map(body, mesh=mesh, in_specs=in_specs, out_specs=out_specs, check_vma=False)
```

profile of v0, /device:TPU:1, one launch (start us, length us, event | category | flops | bytes accessed | tf_op | source)
XLA Modules:
  0.0 315.1 jit_solution(11469307036374939322)
XLA Ops:
  6.5 0.0 copy-start
  6.5 0.0 copy-start.1
  6.5 0.8 fusion.11
  7.3 0.0 copy-done
  7.3 0.7 gather_fusion
  8.0 0.7 copy.37
  8.7 25.0 %all-to-all-start = ((s32[32,1,1]{2,1,0:T(1,128)}), s32[32,1,1]{2,1,0:T(1,128)S(1)}, u32[]{:S(2)}, u32[]{:S(2)}) async-start(s32[32,1,1]{2,1,0:T(1,128)} %copy.37), calls=%async_computation | async-start | bytes 32768 | tf_op jit(solution)/shard_map/all_to_all | solution.py:45
  33.7 0.7 bitcast_compare_fusion
  34.4 0.1 copy.38
  34.5 0.1 broadcast_in_dim.24
  34.7 0.1 reshape.92
  34.8 0.1 broadcast_in_dim.25
  34.9 1.0 copy.40
  35.9 0.0 copy-done.1
  35.9 1.1 bitcast_select_fusion
  37.0 12.8 %all-to-all-done = s32[32,1,1]{2,1,0:T(1,128)S(1)} async-done(((s32[32,1,1]{2,1,0:T(1,128)}), s32[32,1,1]{2,1,0:T(1,128)S(1)}, u32[]{:S(2)}, u32[]{:S(2)}) %all-to-all-start) | async-done | bytes 160 | tf_op jit(solution)/shard_map/all_to_all | solution.py:45
  49.7 3.9 %all-to-all-start.1 = ((bf16[32,128,128]{2,1,0:T(8,128)(2,1)}), bf16[32,128,128]{2,1,0:T(8,128)(2,1)S(1)}, u32[]{:S(2)}, u32[]{:S(2)}) async-start(bf16[32,128,128]{2,1,0:T(8,128)(2,1)} %bitcast_select_fusion), calls=%async_computation.1 | async-start | bytes 2097152 | tf_op jit(solution)/shard_map/all_to_all | solution.py:44
  53.7 0.7 reduce
  54.3 53.2 %all-to-all-done.1 = bf16[32,128,128]{2,1,0:T(8,128)(2,1)S(1)} async-done(((bf16[32,128,128]{2,1,0:T(8,128)(2,1)}), bf16[32,128,128]{2,1,0:T(8,128)(2,1)S(1)}, u32[]{:S(2)}, u32[]{:S(2)}) %all-to-all-start.1) | async-done | bytes 1048608 | tf_op jit(solution)/shard_map/all_to_all | solution.py:44
  107.5 0.7 convolution_convert_fusion
  108.3 1.4 copy.42
  109.7 7.1 %all-to-all-start.2 = ((bf16[32,128,128]{2,1,0:T(8,128)(2,1)}), bf16[32,128,128]{2,1,0:T(8,128)(2,1)S(1)}, u32[]{:S(2)}, u32[]{:S(2)}) async-start(bf16[32,128,128]{2,1,0:T(8,128)(2,1)} %copy.42), calls=%async_computation.2 | async-start | bytes 2097152 | tf_op jit(solution)/shard_map/all_to_all | solution.py:47
  116.8 0.0 all-gather.3.cloned.1.call-start
  116.9 26.5 %all-to-all-done.2 = bf16[32,128,128]{2,1,0:T(8,128)(2,1)S(1)} async-done(((bf16[32,128,128]{2,1,0:T(8,128)(2,1)}), bf16[32,128,128]{2,1,0:T(8,128)(2,1)S(1)}, u32[]{:S(2)}, u32[]{:S(2)}) %all-to-all-start.2) | async-done | bytes 1048608 | tf_op jit(solution)/shard_map/all_to_all | solution.py:47
  143.4 0.7 gather_fusion.1
  144.1 1.3 copy.43
  145.4 1.5 bitcast_add_fusion
  146.9 0.6 constant_dynamic-slice_fusion
  147.6 0.0 all-gather.3.cloned.1.call-update
  147.6 0.0 all-gather.5.cloned.1.call-start
  147.6 0.7 all-gather.5.cloned.1.call-update
  148.3 2.5 collective-permute-start
  150.9 4.2 %collective-permute-start.1 = (s32[32]{0:T(128)S(1)}, s32[32]{0:T(128)S(1)}, u32[]{:S(2)}, u32[]{:S(2)}) collective-permute-start(s32[32]{0:T(128)S(1)} %get-tuple-element.7), channel_id=1, source_target_pairs={{0,31},{1,0},{2,1},{3,2},{4,3},{5,4},{6,5},{7,6},{8,7},{9,8},{10,9... | collective-permute-start | bytes 392 | tf_op jit(solution)/shard_map/ppermute | solution.py:10
  155.1 39.5 %collective-permute-done.1 = s32[32]{0:T(128)S(1)} collective-permute-done((s32[32]{0:T(128)S(1)}, s32[32]{0:T(128)S(1)}, u32[]{:S(2)}, u32[]{:S(2)}) %collective-permute-start.1) | collective-permute-done | bytes 160 | tf_op jit(solution)/shard_map/ppermute | solution.py:10
  194.7 11.4 %all-gather.3.cloned.1.call-done = bf16[32,128,128]{2,1,0:T(8,128)(2,1)} async-done(((bf16[1,128,128]{2,1,0:T(8,128)(2,1)}), bf16[32,128,128]{2,1,0:T(8,128)(2,1)}) %all-gather.3.cloned.1.call-update) | async-done | bytes 1048592 | tf_op jit(solution)/shard_map/all_gather | solution.py:60
  206.1 2.0 gather_fusion.2
  208.0 94.6 %all-gather.5.cloned.1.call-done = bf16[32,128,128]{2,1,0:T(8,128)(2,1)} async-done(((bf16[1,128,128]{2,1,0:T(8,128)(2,1)}), bf16[32,128,128]{2,1,0:T(8,128)(2,1)}) %all-gather.5.cloned.1.call-update) | async-done | bytes 1048592 | tf_op jit(solution)/shard_map/all_gather | solution.py:61
  302.7 2.0 gather_fusion.3
  304.7 0.5 fusion.2
  305.2 0.0 collective-permute-done
  305.2 3.1 add_bitcast_fusion
  (9 shorter events, 0.1 us)
Async XLA Ops:
  6.5 0.8 copy-start
  6.5 29.4 %copy-start.1 = (bf16[1,1,32,128,128]{4,3,2,1,0:T(8,128)(2,1)S(1)}, bf16[1,1,32,128,128]{4,3,2,1,0:T(8,128)(2,1)}, u32[]{:S(2)}) copy-start(bf16[1,1,32,128,128]{4,3,2,1,0:T(8,128)(2,1)} %param.6) | copy-start | bytes 3145732
  8.7 41.0 %all-to-all-start = ((s32[32,1,1]{2,1,0:T(1,128)}), s32[32,1,1]{2,1,0:T(1,128)S(1)}, u32[]{:S(2)}, u32[]{:S(2)}) async-start(s32[32,1,1]{2,1,0:T(1,128)} %copy.37), calls=%async_computation | async-start | bytes 32768 | tf_op jit(solution)/shard_map/all_to_all | solution.py:45
  49.7 57.8 %all-to-all-start.1 = ((bf16[32,128,128]{2,1,0:T(8,128)(2,1)}), bf16[32,128,128]{2,1,0:T(8,128)(2,1)S(1)}, u32[]{:S(2)}, u32[]{:S(2)}) async-start(bf16[32,128,128]{2,1,0:T(8,128)(2,1)} %bitcast_select_fusion), calls=%async_computation.1 | async-start | bytes 2097152 | tf_op jit(solution)/shard_map/all_to_all | solution.py:44
  109.7 33.7 %all-to-all-start.2 = ((bf16[32,128,128]{2,1,0:T(8,128)(2,1)}), bf16[32,128,128]{2,1,0:T(8,128)(2,1)S(1)}, u32[]{:S(2)}, u32[]{:S(2)}) async-start(bf16[32,128,128]{2,1,0:T(8,128)(2,1)} %copy.42), calls=%async_computation.2 | async-start | bytes 2097152 | tf_op jit(solution)/shard_map/all_to_all | solution.py:47
  116.8 89.3 %all-gather.3.cloned.1.call-start = ((), (), s32[]{:S(2)}) async-start(), calls=%async_computation.3 | async-start | bytes 1081344 | tf_op jit(solution)/shard_map/all_gather | solution.py:60
  147.6 155.1 %all-gather.5.cloned.1.call-start = ((), (), s32[]{:S(2)}) async-start(), calls=%async_computation.4 | async-start | bytes 1081344 | tf_op jit(solution)/shard_map/all_gather | solution.py:61
  148.3 156.8 %collective-permute-start = (bf16[32,128,128]{2,1,0:T(8,128)(2,1)S(1)}, bf16[32,128,128]{2,1,0:T(8,128)(2,1)}, u32[]{:S(2)}, u32[]{:S(2)}) collective-permute-start(bf16[32,128,128]{2,1,0:T(8,128)(2,1)S(1)} %bitcast_add_fusion), channel_id=1, source_target_pairs={{0,31},{1,0},{2,1},{3,2},{4,3},{5,4},{6,5},{7,6},{8,7},{9,8},{10,9... | collective-permute-start | bytes 3145736 | tf_op jit(solution)/shard_map/ppermute | solution.py:10
  150.9 43.8 %collective-permute-start.1 = (s32[32]{0:T(128)S(1)}, s32[32]{0:T(128)S(1)}, u32[]{:S(2)}, u32[]{:S(2)}) collective-permute-start(s32[32]{0:T(128)S(1)} %get-tuple-element.7), channel_id=1, source_target_pairs={{0,31},{1,0},{2,1},{3,2},{4,3},{5,4},{6,5},{7,6},{8,7},{9,8},{10,9... | collective-permute-start | bytes 392 | tf_op jit(solution)/shard_map/ppermute | solution.py:10
Sparse Core Ops, SparseCore 0:
  147.7 58.3 all-gather.2
  208.8 93.8 all-gather.4
where the time goes:
time: 316 us; the launch traced here: 315 us
  waiting for transfers between devices  239 us (76%)
  starting transfers between devices  42.9 us (14%)
  between operations  13.6 us (4%)
  local copies, waits for them, and re-layouts  10.9 us (3%)
  other arithmetic  4.74 us (2%)
  matrix products  4.34 us (1%)
    all_gather x1, waiting for transfers between devices, body(): lax.all_gather(ahead_group, 'row', axis=0, tiled=True)  94.6 us
    all_to_all x1, waiting for transfers between devices, body(): lax.all_to_all(outgoing, 'col', split_axis=0, concat_axis=0, tiled=True)  53.2 us
    ppermute x2, waiting for transfers between devices, passed_along(): return lax.ppermute(value, axis, pairs)  39.5 us
    all_to_all x1, waiting for transfers between devices, body(): lax.all_to_all(to_buckets(arrived, arrived_rows, rows_count), 'row', spli...  26.5 us
    all_to_all x1, starting transfers between devices, body(): lax.all_to_all(partner, 'col', split_axis=0, concat_axis=0, tiled=True)  25 us
    all_to_all x1, waiting for transfers between devices, body(): lax.all_to_all(partner, 'col', split_axis=0, concat_axis=0, tiled=True)  12.8 us
    all_gather x1, waiting for transfers between devices, body(): lax.all_gather(diagonal, 'row', axis=0, tiled=True)  11.4 us
    all_to_all x1, starting transfers between devices, body(): lax.all_to_all(to_buckets(arrived, arrived_rows, rows_count), 'row', spli...  7.11 us
  transfers between devices with their start and end apart: 7, of which 6 were waited for; matrix products, arithmetic and copies ran while one was open for 3% of the time, Pallas kernels for 0%

commit v1 on v0

v1 whole, which is shorter than its diff:
```python
import functools

import jax
import jax.numpy as jnp
from jax import lax
from jax.experimental import pallas as pl
from jax.experimental.pallas import tpu as pltpu
from jax.sharding import PartitionSpec as P

MESH = pl.DeviceIdType.MESH

ROW_SPLIT = (4, 4, 2)
COL_SPLIT = (2, 16)
CHUNKS = 4


def kernel(
    row_split, col_split, chunks, jc_ref, inv_ref, stored_ref, out_ref, turned, gathered, ahead, total, total_next, *rest
):
    landed, buckets, mirrored = rest[:chunks], rest[chunks : 2 * chunks], rest[2 * chunks : 3 * chunks]
    send_sem, m_sem, g_sem, a_sem, b_sem, w_sem = rest[3 * chunks :]
    ny, nx, ncore = row_split
    nhi, nz = col_split
    nr, nc = ny * nx * ncore, nhi * nz
    width = stored_ref.shape[-1]
    strip = width // chunks
    r, c = lax.axis_index("row"), lax.axis_index("col")
    core, x, y = lax.rem(r, ncore), lax.rem(r // ncore, nx), r // (ncore * nx)
    z, hi = lax.rem(c, nz), c // nz
    following, previous = lax.rem(c + 1, nc), lax.rem(c + nc - 1, nc)

    def remote(src, dst, slot, recv, **where):
        return pltpu.make_async_remote_copy(
            src_ref=src,
            dst_ref=dst,
            send_sem=send_sem.at[slot],
            recv_sem=recv,
            device_id=where,
            device_id_type=MESH,
        )

    barrier = pltpu.get_barrier_semaphore()

    def greet_col(t, carry):
        pl.semaphore_signal(barrier, inc=1, device_id={"col": lax.rem(c + t, nc)}, device_id_type=MESH)
        return carry

    def greet_row(t, carry):
        pl.semaphore_signal(barrier, inc=1, device_id={"row": lax.rem(r + t, nr)}, device_id_type=MESH)
        return carry

    lax.fori_loop(1, nc, greet_col, 0)
    lax.fori_loop(1, nr, greet_row, 0)

    def turn(t, carry):
        turned[t] = stored_ref[t].T
        return carry

    lax.fori_loop(0, nc, turn, 0, unroll=2)

    half = width // 2
    rows = lax.broadcasted_iota(jnp.int32, (width, width), 0)
    cols = lax.broadcasted_iota(jnp.int32, (width, width), 1)
    own = stored_ref[c].astype(jnp.float32)
    flipped = turned[c].astype(jnp.float32)
    diagonal = (own + jnp.where((rows >= half) != (cols >= half), flipped, 0.0)).astype(jnp.bfloat16)
    gathered[y, x, core, 0] = diagonal
    gathered[y, x, core, 1] = stored_ref[following]
    total[0] = diagonal

    pl.semaphore_wait(barrier, nc + nr - 2)

    ahead_copy = remote(
        turned.at[previous], gathered.at[y, x, core, 2], 0, m_sem.at[0], col=previous
    )
    ahead_copy.start()

    def offset_col(t):
        m = t // nhi
        sign = 2 * lax.rem(m, 2) - 1
        return lax.rem(hi + lax.rem(t, nhi), nhi) * nz + lax.rem(z + sign * ((m + 1) // 2) + nz, nz)

    for k in range(chunks):
        rows_k = pl.ds(k * strip, strip)

        def send_col(s, carry, k=k, rows_k=rows_k):
            to = offset_col(nc - s)
            remote(turned.at[to, rows_k], landed[k].at[c], 1, a_sem.at[k], col=to).start()
            return carry

        lax.fori_loop(1, nc, send_col, 0)

    ahead_copy.wait_recv()
    mine = gathered.at[y, x, core]
    for s in range(1, ny):
        remote(mine, mine, 4 + s, g_sem.at[s], row=(lax.rem(y + s, ny) * nx + x) * ncore + core).start()

    def gather_x():
        for s in range(1, ny):
            remote(mine, mine, 4 + s, g_sem.at[s], row=r).wait_recv()
        line = gathered.at[:, x, core]
        for s in range(1, nx):
            remote(line, line, 4 + ny + s, g_sem.at[ny + s], row=(y * nx + lax.rem(x + s, nx)) * ncore + core).start()

    def gather_core():
        line = gathered.at[:, x, core]
        for s in range(1, nx):
            remote(line, line, 4 + ny + s, g_sem.at[ny + s], row=r).wait_recv()
        plane = gathered.at[:, :, core]
        for s in range(1, ncore):
            remote(plane, plane, 4 + ny + nx + s, g_sem.at[ny + nx + s], row=(y * nx + x) * ncore + lax.rem(core + s, ncore)).start()

    for k in range(chunks):
        rows_k = pl.ds(k * strip, strip)
        remote(landed[k].at[pl.ds(1, nc - 1)], landed[k].at[pl.ds(1, nc - 1)], 1, a_sem.at[k], row=r).wait_recv()

        def send_row(t, carry, k=k):
            j = nr // 2 + (2 * lax.rem(t, 2) - 1) * ((t + 1) // 2)
            buckets[k][j] = landed[k][inv_ref[j]]
            remote(buckets[k].at[j], mirrored[k].at[j], 2, b_sem.at[k], row=lax.rem(r + j, nr)).start()
            return carry

        lax.fori_loop(0, nr - 1, send_row, 0)
        if k == 0:
            gather_x()
        if k == min(1, chunks - 1):
            gather_core()
        remote(mirrored[k].at[pl.ds(1, nr - 1)], mirrored[k].at[pl.ds(1, nr - 1)], 2, b_sem.at[k], row=r).wait_recv()

        def complete(j, carry, k=k, rows_k=rows_k):
            total[j, rows_k] = stored_ref[inv_ref[j], rows_k] + mirrored[k][j]
            return carry

        lax.fori_loop(1, nr, complete, 0)
        remote(total.at[:, rows_k], total_next.at[:, rows_k], 3, w_sem.at[k], col=previous).start()

    plane = gathered.at[:, :, core]
    for s in range(1, ncore):
        remote(plane, plane, 4 + ny + nx + s, g_sem.at[ny + nx + s], row=r).wait_recv()
    shift = jc_ref[following]

    def place(row):
        row = lax.rem(row + 2 * nr, nr)
        return row // (ncore * nx), lax.rem(row // ncore, nx), lax.rem(row, ncore)

    def fill_ahead(p, carry):
        here, there = place(p), place(p - shift)
        ahead[p] = gathered[here[0], here[1], here[2], 1] + gathered[there[0], there[1], there[2], 2]
        return carry

    lax.fori_loop(0, nr, fill_ahead, 0)

    def diag_term(t, carry):
        j = jc_ref[t]
        at = place(r - j)
        out_ref[t] = jnp.dot(total[j], gathered[at[0], at[1], at[2], 0], preferred_element_type=jnp.float32)
        return carry

    lax.fori_loop(0, nc, diag_term, 0, unroll=2)
    for k in range(chunks):
        rows_k = pl.ds(k * strip, strip)
        remote(total.at[:, rows_k], total_next.at[:, rows_k], 3, w_sem.at[k], col=previous).wait_recv()

    def ahead_term(t, carry):
        j = lax.rem(jc_ref[t] - shift + nr, nr)
        out_ref[t] += jnp.dot(
            total_next[j], ahead[lax.rem(r - j + nr, nr)], preferred_element_type=jnp.float32
        )
        return carry

    lax.fori_loop(0, nc, ahead_term, 0, unroll=2)

    ahead_copy.wait_send()
    remote(turned.at[pl.ds(1, nc - 1)], turned.at[pl.ds(1, nc - 1)], 1, m_sem.at[0], row=r).wait_send()
    for s in range(1, ny):
        remote(mine, mine, 4 + s, g_sem.at[s], row=r).wait_send()
    line = gathered.at[:, x, core]
    for s in range(1, nx):
        remote(line, line, 4 + ny + s, g_sem.at[ny + s], row=r).wait_send()
    for s in range(1, ncore):
        remote(plane, plane, 4 + ny + nx + s, g_sem.at[ny + nx + s], row=r).wait_send()
    remote(turned.at[pl.ds(1, nr - 1)], turned.at[pl.ds(1, nr - 1)], 2, m_sem.at[0], row=r).wait_send()
    remote(total, total, 3, m_sem.at[0], row=r).wait_send()


def body(row_split, col_split, chunks, stored, pair_rows, pair_cols, block_owner):
    nr, nc = lax.axis_size("row"), lax.axis_size("col")
    places = pair_rows.shape[-1]
    width = stored.shape[-1]
    strip = width // chunks
    partner = block_owner[pair_cols[0, 0, :, 0, 0]] // (nc * places)
    jc = lax.rem(lax.axis_index("row") - partner + nr, nr)
    slots = lax.broadcasted_iota(jnp.int32, (nr, nc), 1)
    inv = jnp.sum(jnp.where(jc[None, :] == jnp.arange(nr, dtype=jnp.int32)[:, None], slots, 0), axis=1)
    groups = jax.ShapeDtypeStruct((nc, width, width), jnp.bfloat16)
    vmem = lambda *shape: pltpu.VMEM(shape, jnp.bfloat16)
    smem_spec = pl.BlockSpec(memory_space=pltpu.SMEM)
    vmem_spec = pl.BlockSpec(memory_space=pltpu.VMEM)
    out = pl.pallas_call(
        functools.partial(kernel, row_split, col_split, chunks),
        out_shape=jax.ShapeDtypeStruct((nc, width, width), jnp.float32),
        in_specs=[smem_spec, smem_spec, vmem_spec],
        out_specs=vmem_spec,
        scratch_shapes=[
            vmem(nc, width, width),
            vmem(*row_split, 3, width, width),
            vmem(nr, width, width),
            vmem(nr, width, width),
            vmem(nr, width, width),
            *[vmem(nc, strip, width) for _ in range(chunks)],
            *[vmem(nr, strip, width) for _ in range(chunks)],
            *[vmem(nr, strip, width) for _ in range(chunks)],
            pltpu.SemaphoreType.DMA((4 + sum(row_split),)),
            pltpu.SemaphoreType.DMA((1,)),
            pltpu.SemaphoreType.DMA((sum(row_split),)),
            pltpu.SemaphoreType.DMA((chunks,)),
            pltpu.SemaphoreType.DMA((chunks,)),
            pltpu.SemaphoreType.DMA((chunks,)),
        ],
        compiler_params=pltpu.CompilerParams(
            collective_id=0, has_side_effects=True, vmem_limit_bytes=40 * 1024 * 1024
        ),
    )(jc, inv, stored[0, 0])
    return out[None, None]


def build(mesh, row_split, col_split, chunks):
    in_specs = (
        P("row", "col", None, None, None),
        P("row", "col", None, None, None),
        P("row", "col", None, None, None),
        P(),
    )
    out_specs = P("row", "col", None, None, None)
    run = functools.partial(body, row_split, col_split, chunks)
    return jax.shard_map(run, mesh=mesh, in_specs=in_specs, out_specs=out_specs, check_vma=False)


def solution(mesh):
    return build(mesh, ROW_SPLIT, COL_SPLIT, CHUNKS)
```

time: 316 us -> 137 us (0.43)
  the two profiles are of different devices: /device:TPU:1 before, /device:TPU:896 now
where the time goes in v1:
time: 137 us
  Pallas kernels  133 us (97%)
  local copies, waits for them, and re-layouts  3.25 us (2%)
    pallas_call x1, Pallas kernels, body(): pl.pallas_call(functools.partial(kernel, row_split, col_split, chunks), o...  133 us

profile of v1, /device:TPU:896, one launch (start us, length us, event | category | flops | bytes accessed | tf_op | source)
XLA Modules:
  0.0 137.2 jit_solution(6879525377458008579)
XLA Ops:
  0.0 0.0 copy-start
  0.0 0.7 fusion.1
  0.7 0.0 copy-done
  0.7 0.7 gather_fusion
  1.4 0.1 select_reduce_fusion.inv_ref
  1.5 0.0 copy-start.1
  1.6 1.2 copy-done.1
  2.8 133.1 %shard_map.37 = f32[32,128,128]{2,1,0:T(8,128)S(1)} custom-call(s32[32]{0:T(128)S(1)} %compare_select_fusion.1.jc_ref, s32[32]{0:T(128)S(1)} %select_reduce_fusion.inv_ref, bf16[32,128,128]{2,1,0:T(8,128)(2,1)S(1)} %bitcast.7), custom_call_target="tpu_custom_call" | custom-call | tf_op jit(solution)/shard_map/pallas_call | solution.py:199
  135.9 1.3 copy.5
  (2 shorter events, 0.0 us)
Async XLA Ops:
  0.0 0.7 copy-start
  1.5 1.2 copy-start.1

commit v2 on v1

v2 whole, which is shorter than its diff:
```python
import functools

import jax
import jax.numpy as jnp
from jax import lax
from jax.experimental import pallas as pl
from jax.experimental.pallas import tpu as pltpu
from jax.sharding import PartitionSpec as P

MESH = pl.DeviceIdType.MESH

ROW_SPLIT = (4, 4, 2)
COL_SPLIT = (2, 16)
STRIPS = (32, 32, 32, 32)
CROSSINGS = ((15, 8), (14, 8), (13, 8), (12, 8))


def kernel(
    row_split, col_split, strips, crossings, jc_ref, inv_ref, stored_ref, out_ref, turned, gathered, ahead, total, total_next, relayed, *rest
):
    chunks = len(strips)
    starts = [sum(strips[:k]) for k in range(chunks)]
    landed, buckets, mirrored = rest[:chunks], rest[chunks : 2 * chunks], rest[2 * chunks : 3 * chunks]
    send_sem, m_sem, g_sem, a_sem, b_sem, w_sem, r_sem = rest[3 * chunks :]
    ny, nx, ncore = row_split
    nhi, nz = col_split
    nr, nc = ny * nx * ncore, nhi * nz
    width = stored_ref.shape[-1]
    r, c = lax.axis_index("row"), lax.axis_index("col")
    core, x, y = lax.rem(r, ncore), lax.rem(lax.div(r, ncore), nx), lax.div(r, ncore * nx)
    z, hi = lax.rem(c, nz), lax.div(c, nz)
    following, previous = lax.rem(c + 1, nc), lax.rem(c + nc - 1, nc)

    def remote(src, dst, slot, recv, **where):
        return pltpu.make_async_remote_copy(
            src_ref=src,
            dst_ref=dst,
            send_sem=send_sem.at[slot],
            recv_sem=recv,
            device_id=where,
            device_id_type=MESH,
        )

    barrier = pltpu.get_barrier_semaphore()

    def greet_col(t, carry):
        pl.semaphore_signal(barrier, inc=1, device_id={"col": lax.rem(c + t, nc)}, device_id_type=MESH)
        return carry

    def greet_row(t, carry):
        pl.semaphore_signal(barrier, inc=1, device_id={"row": lax.rem(r + t, nr)}, device_id_type=MESH)
        return carry

    lax.fori_loop(1, nc, greet_col, 0)
    lax.fori_loop(1, nr, greet_row, 0)

    def turn(t, carry):
        turned[t] = stored_ref[t].T
        return carry

    lax.fori_loop(0, nc, turn, 0, unroll=2)

    half = width // 2
    rows = lax.broadcasted_iota(jnp.int32, (width, width), 0)
    cols = lax.broadcasted_iota(jnp.int32, (width, width), 1)
    own = stored_ref[c].astype(jnp.float32)
    flipped = turned[c].astype(jnp.float32)
    diagonal = (own + jnp.where((rows >= half) != (cols >= half), flipped, 0.0)).astype(jnp.bfloat16)
    gathered[y, x, core, 0] = diagonal
    gathered[y, x, core, 1] = stored_ref[following]
    total[0] = diagonal

    pl.semaphore_wait(barrier, nc + nr - 2)

    ahead_copy = remote(
        turned.at[previous], gathered.at[y, x, core, 2], 0, m_sem.at[0], col=previous
    )
    ahead_copy.start()

    here, other = hi * nz, (nhi - 1 - hi) * nz
    far = nz // 2

    def send_to(k, to):
        rows_k = pl.ds(starts[k], strips[k])
        remote(turned.at[to, rows_k], landed[k].at[c], 1, a_sem.at[k], col=to).start()

    def send_cols(k):
        up, down = lax.rem(z + far - 1, nz), lax.rem(z + far + 1, nz)
        send_to(k, here + lax.rem(z + far, nz))
        send_to(k, other + lax.rem(z + far, nz))
        send_to(k, here + down)
        send_to(k, here + up)
        send_to(k, other + down)
        send_to(k, other + up)

        def send_pairs(s, carry):
            m = far - s
            up, down = lax.rem(z + m, nz), lax.rem(z + nz - m, nz)
            send_to(k, here + up)
            send_to(k, other + down)
            send_to(k, other + up)
            send_to(k, here + down)
            return carry

        lax.fori_loop(2, far, send_pairs, 0)
        send_to(k, other + z)

    send_cols(0)
    ahead_copy.wait_recv()
    mine = gathered.at[y, x, core]
    for s in range(1, ny):
        remote(mine, mine, 7 + s, g_sem.at[s], row=(lax.rem(y + s, ny) * nx + x) * ncore + core).start()

    for k in range(1, chunks):
        send_cols(k)

    def gather_x():
        for s in range(1, ny):
            remote(mine, mine, 7 + s, g_sem.at[s], row=r).wait_recv()
        line = gathered.at[:, x, core]
        for s in range(1, nx):
            remote(line, line, 7 + ny + s, g_sem.at[ny + s], row=(y * nx + lax.rem(x + s, nx)) * ncore + core).start()

    def gather_core():
        line = gathered.at[:, x, core]
        for s in range(1, nx):
            remote(line, line, 7 + ny + s, g_sem.at[ny + s], row=r).wait_recv()
        plane = gathered.at[:, :, core]
        for s in range(1, ncore):
            remote(plane, plane, 7 + ny + nx + s, g_sem.at[ny + nx + s], row=(y * nx + x) * ncore + lax.rem(core + s, ncore)).start()

    def parts():
        start = 0
        for plane, count in crossings:
            yield plane, pl.ds(start, count), pl.ds(0, count)
            start += count

    def shift_on(k):
        rows_k = pl.ds(starts[k], strips[k])

        @pl.when(z != 0)
        def _():
            remote(total.at[:, rows_k], total_next.at[:, rows_k], 3, w_sem.at[k], col=previous).start()

        @pl.when(z == 0)
        def _():
            for plane, part, slots in parts():
                to = lax.rem(hi + nhi - 1, nhi) * nz + plane
                if plane == nz - 1:
                    dst, sem = total_next.at[part, rows_k], w_sem.at[k]
                else:
                    dst, sem = relayed.at[slots, rows_k], r_sem.at[k]
                remote(total.at[part, rows_k], dst, 3, sem, col=to).start()

    def relay_on(k):
        rows_k = pl.ds(starts[k], strips[k])
        for plane, part, slots in parts():
            if plane != nz - 1:

                @pl.when(z == plane)
                def _(part=part, slots=slots):
                    src, dst = relayed.at[slots, rows_k], total_next.at[part, rows_k]
                    remote(src, src, 3, r_sem.at[k], row=r).wait_recv()
                    remote(src, dst, 5, w_sem.at[k], col=hi * nz + nz - 1).start()

    for k in range(chunks):
        rows_k = pl.ds(starts[k], strips[k])
        remote(landed[k].at[pl.ds(1, nc - 1)], landed[k].at[pl.ds(1, nc - 1)], 1, a_sem.at[k], row=r).wait_recv()

        def send_row(j, k=k):
            buckets[k][j] = landed[k][inv_ref[j]]
            remote(buckets[k].at[j], mirrored[k].at[j], 2, b_sem.at[k], row=lax.rem(r + j, nr)).start()

        def send_rows(s, carry):
            send_row(nr // 2 - s)
            send_row(nr // 2 + s)
            return carry

        send_row(nr // 2)
        lax.fori_loop(1, nr // 2, send_rows, 0)
        if k == 0:
            gather_x()
        if k == min(1, chunks - 1):
            gather_core()
        if k > 0:
            relay_on(k - 1)
        remote(mirrored[k].at[pl.ds(1, nr - 1)], mirrored[k].at[pl.ds(1, nr - 1)], 2, b_sem.at[k], row=r).wait_recv()

        def complete(j, carry, k=k, rows_k=rows_k):
            total[j, rows_k] = stored_ref[inv_ref[j], rows_k] + mirrored[k][j]
            return carry

        lax.fori_loop(1, nr, complete, 0)
        shift_on(k)

    relay_on(chunks - 1)
    plane = gathered.at[:, :, core]
    for s in range(1, ncore):
        remote(plane, plane, 7 + ny + nx + s, g_sem.at[ny + nx + s], row=r).wait_recv()
    shift = jc_ref[following]

    def place(row):
        row = lax.rem(row + 2 * nr, nr)
        return lax.div(row, ncore * nx), lax.rem(lax.div(row, ncore), nx), lax.rem(row, ncore)

    def fill_ahead(p, carry):
        here, there = place(p), place(p - shift)
        ahead[p] = gathered[here[0], here[1], here[2], 1] + gathered[there[0], there[1], there[2], 2]
        return carry

    lax.fori_loop(0, nr, fill_ahead, 0)

    def diag_term(t, carry):
        j = jc_ref[t]
        at = place(r - j)
        out_ref[t] = jnp.dot(total[j], gathered[at[0], at[1], at[2], 0], preferred_element_type=jnp.float32)
        return carry

    lax.fori_loop(0, nc, diag_term, 0, unroll=2)
    for k in range(chunks):
        rows_k = pl.ds(starts[k], strips[k])
        remote(total.at[:, rows_k], total_next.at[:, rows_k], 3, w_sem.at[k], col=previous).wait_recv()

    def ahead_term(t, carry):
        j = lax.rem(jc_ref[t] - shift + nr, nr)
        out_ref[t] += jnp.dot(
            total_next[j], ahead[lax.rem(r - j + nr, nr)], preferred_element_type=jnp.float32
        )
        return carry

    lax.fori_loop(0, nc, ahead_term, 0, unroll=2)

    ahead_copy.wait_send()
    sent = turned.at[pl.ds(0, nc - 1)]
    remote(sent, sent, 1, m_sem.at[0], row=r).wait_send()
    for s in range(1, ny):
        remote(mine, mine, 7 + s, g_sem.at[s], row=r).wait_send()
    line = gathered.at[:, x, core]
    for s in range(1, nx):
        remote(line, line, 7 + ny + s, g_sem.at[ny + s], row=r).wait_send()
    for s in range(1, ncore):
        remote(plane, plane, 7 + ny + nx + s, g_sem.at[ny + nx + s], row=r).wait_send()
    remote(turned.at[pl.ds(1, nr - 1)], turned.at[pl.ds(1, nr - 1)], 2, m_sem.at[0], row=r).wait_send()
    remote(total, total, 3, m_sem.at[0], row=r).wait_send()
    for between, _, slots in parts():
        if between != nz - 1:

            @pl.when(z == between)
            def _(slots=slots):
                remote(relayed.at[slots], relayed.at[slots], 5, m_sem.at[0], row=r).wait_send()


def body(row_split, col_split, strips, crossings, stored, pair_rows, pair_cols, block_owner):
    nr, nc = lax.axis_size("row"), lax.axis_size("col")
    places = pair_rows.shape[-1]
    width = stored.shape[-1]
    chunks = len(strips)
    partner = block_owner[pair_cols[0, 0, :, 0, 0]] // (nc * places)
    jc = lax.rem(lax.axis_index("row") - partner + nr, nr)
    slots = lax.broadcasted_iota(jnp.int32, (nr, nc), 1)
    inv = jnp.sum(jnp.where(jc[None, :] == jnp.arange(nr, dtype=jnp.int32)[:, None], slots, 0), axis=1)
    groups = jax.ShapeDtypeStruct((nc, width, width), jnp.bfloat16)
    vmem = lambda *shape: pltpu.VMEM(shape, jnp.bfloat16)
    smem_spec = pl.BlockSpec(memory_space=pltpu.SMEM)
    vmem_spec = pl.BlockSpec(memory_space=pltpu.VMEM)
    out = pl.pallas_call(
        functools.partial(kernel, row_split, col_split, strips, crossings),
        out_shape=jax.ShapeDtypeStruct((nc, width, width), jnp.float32),
        in_specs=[smem_spec, smem_spec, vmem_spec],
        out_specs=vmem_spec,
        scratch_shapes=[
            vmem(nc, width, width),
            vmem(*row_split, 3, width, width),
            vmem(nr, width, width),
            vmem(nr, width, width),
            vmem(nr, width, width),
            vmem(max(count for _, count in crossings), width, width),
            *[vmem(nc, strip, width) for strip in strips],
            *[vmem(nr, strip, width) for strip in strips],
            *[vmem(nr, strip, width) for strip in strips],
            pltpu.SemaphoreType.DMA((7 + sum(row_split),)),
            pltpu.SemaphoreType.DMA((1,)),
            pltpu.SemaphoreType.DMA((sum(row_split),)),
            pltpu.SemaphoreType.DMA((chunks,)),
            pltpu.SemaphoreType.DMA((chunks,)),
            pltpu.SemaphoreType.DMA((chunks,)),
            pltpu.SemaphoreType.DMA((chunks,)),
        ],
        compiler_params=pltpu.CompilerParams(
            collective_id=0, has_side_effects=True, vmem_limit_bytes=40 * 1024 * 1024
        ),
    )(jc, inv, stored[0, 0])
    return out[None, None]


def build(mesh, row_split, col_split, strips, crossings):
    in_specs = (
        P("row", "col", None, None, None),
        P("row", "col", None, None, None),
        P("row", "col", None, None, None),
        P(),
    )
    out_specs = P("row", "col", None, None, None)
    run = functools.partial(body, row_split, col_split, strips, crossings)
    return jax.shard_map(run, mesh=mesh, in_specs=in_specs, out_specs=out_specs, check_vma=False)


def solution(mesh):
    return build(mesh, ROW_SPLIT, COL_SPLIT, STRIPS, CROSSINGS)
```

time: 137 us -> 106 us (0.77)
  the two profiles are of different devices: /device:TPU:896 before, /device:TPU:1 now
where the time goes in v2:
time: 106 us; the launch traced here: 104 us
  Pallas kernels  99.4 us (94%)
  local copies, waits for them, and re-layouts  3.25 us (3%)
    pallas_call x1, Pallas kernels, body(): pl.pallas_call(functools.partial(kernel, row_split, col_split, strips, cr...  99.4 us
    unnamed x5, local copies, waits for them, and re-layouts  2.55 us

profile of v2, /device:TPU:1, one launch (start us, length us, event | category | flops | bytes accessed | tf_op | source)
XLA Modules:
  0.0 103.5 jit_solution(4226078422973198110)
XLA Ops:
  0.0 0.0 copy-start
  0.0 0.7 fusion.1
  0.7 0.0 copy-done
  0.7 0.7 gather_fusion
  1.4 0.1 select_reduce_fusion.inv_ref
  1.5 0.0 copy-start.1
  1.6 1.2 %copy-done.1 = bf16[1,1,32,128,128]{4,3,2,1,0:T(8,128)(2,1)S(1)} copy-done((bf16[1,1,32,128,128]{4,3,2,1,0:T(8,128)(2,1)S(1)}, bf16[1,1,32,128,128]{4,3,2,1,0:T(8,128)(2,1)}, u32[]{:S(2)}) %copy-start.1) | copy-done | bytes 1048600
  2.8 99.4 %shard_map.37 = f32[32,128,128]{2,1,0:T(8,128)S(1)} custom-call(s32[32]{0:T(128)S(1)} %compare_select_fusion.1.jc_ref, s32[32]{0:T(128)S(1)} %select_reduce_fusion.inv_ref, bf16[32,128,128]{2,1,0:T(8,128)(2,1)S(1)} %bitcast.7), custom_call_target="tpu_custom_call" | custom-call | tf_op jit(solution)/shard_map/pallas_call | solution.py:266
  102.2 1.3 %copy.5 = f32[1,1,32,128,128]{4,3,2,1,0:T(8,128)} copy(f32[1,1,32,128,128]{4,3,2,1,0:T(8,128)S(1)} %bitcast.6) | data formatting | bytes 4194304
  (2 shorter events, 0.0 us)
Async XLA Ops:
  0.0 0.7 copy-start
  1.5 1.2 %copy-start.1 = (bf16[1,1,32,128,128]{4,3,2,1,0:T(8,128)(2,1)S(1)}, bf16[1,1,32,128,128]{4,3,2,1,0:T(8,128)(2,1)}, u32[]{:S(2)}) copy-start(bf16[1,1,32,128,128]{4,3,2,1,0:T(8,128)(2,1)} %param.4) | copy-start | bytes 3145732

commit v3 on v2

--- a/solution.py
+++ b/solution.py
@@ -12,7 +12,7 @@
 ROW_SPLIT = (4, 4, 2)
 COL_SPLIT = (2, 16)
 STRIPS = (32, 32, 32, 32)
-CROSSINGS = ((15, 8), (14, 8), (13, 8), (12, 8))
+CROSSINGS = ((15, 8), (14, 6), (13, 6), (12, 6), (11, 6))
 
 
 def kernel(

time: 106 us -> 104 us (0.981); the launches traced: 104 us -> 104 us
  no operation moved by 1% of the time
where the time goes in v3:
time: 104 us
  Pallas kernels  99.4 us (96%)
  local copies, waits for them, and re-layouts  3.25 us (3%)
    pallas_call x1, Pallas kernels, body(): pl.pallas_call(functools.partial(kernel, row_split, col_split, strips, cr...  99.4 us
    unnamed x5, local copies, waits for them, and re-layouts  2.55 us

profile of v3, /device:TPU:1, one launch (start us, length us, event | category | flops | bytes accessed | tf_op | source)
XLA Modules:
  0.0 103.5 jit_solution(3674467779643354000)
XLA Ops:
  0.0 0.0 copy-start
  0.0 0.7 fusion.1
  0.7 0.0 copy-done
  0.7 0.7 gather_fusion
  1.4 0.1 select_reduce_fusion.inv_ref
  1.5 0.0 copy-start.1
  1.6 1.2 %copy-done.1 = bf16[1,1,32,128,128]{4,3,2,1,0:T(8,128)(2,1)S(1)} copy-done((bf16[1,1,32,128,128]{4,3,2,1,0:T(8,128)(2,1)S(1)}, bf16[1,1,32,128,128]{4,3,2,1,0:T(8,128)(2,1)}, u32[]{:S(2)}) %copy-start.1) | copy-done | bytes 1048600
  2.8 99.4 %shard_map.37 = f32[32,128,128]{2,1,0:T(8,128)S(1)} custom-call(s32[32]{0:T(128)S(1)} %compare_select_fusion.1.jc_ref, s32[32]{0:T(128)S(1)} %select_reduce_fusion.inv_ref, bf16[32,128,128]{2,1,0:T(8,128)(2,1)S(1)} %bitcast.7), custom_call_target="tpu_custom_call" | custom-call | tf_op jit(solution)/shard_map/pallas_call | solution.py:266
  102.2 1.3 %copy.5 = f32[1,1,32,128,128]{4,3,2,1,0:T(8,128)} copy(f32[1,1,32,128,128]{4,3,2,1,0:T(8,128)S(1)} %bitcast.6) | data formatting | bytes 4194304
  (2 shorter events, 0.0 us)
Async XLA Ops:
  0.0 0.7 copy-start
  1.5 1.2 %copy-start.1 = (bf16[1,1,32,128,128]{4,3,2,1,0:T(8,128)(2,1)S(1)}, bf16[1,1,32,128,128]{4,3,2,1,0:T(8,128)(2,1)}, u32[]{:S(2)}) copy-start(bf16[1,1,32,128,128]{4,3,2,1,0:T(8,128)(2,1)} %param.4) | copy-start | bytes 3145732

commit v4 on v3

--- a/solution.py
+++ b/solution.py
@@ -12,7 +12,7 @@
 ROW_SPLIT = (4, 4, 2)
 COL_SPLIT = (2, 16)
 STRIPS = (32, 32, 32, 32)
-CROSSINGS = ((15, 8), (14, 6), (13, 6), (12, 6), (11, 6))
+CROSSINGS = ((15, 7), (14, 5), (13, 5), (12, 5), (11, 5), (10, 5))
 
 
 def kernel(

time: 104 us -> 104 us (level)
  no operation moved by 1% of the time
where the time goes in v4:
time: 104 us
  Pallas kernels  99.4 us (96%)
  local copies, waits for them, and re-layouts  3.25 us (3%)
    pallas_call x1, Pallas kernels, body(): pl.pallas_call(functools.partial(kernel, row_split, col_split, strips, cr...  99.4 us
    unnamed x5, local copies, waits for them, and re-layouts  2.55 us

profile of v4, /device:TPU:1, one launch (start us, length us, event | category | flops | bytes accessed | tf_op | source)
XLA Modules:
  0.0 103.5 jit_solution(12712840134820818104)
XLA Ops:
  0.0 0.0 copy-start
  0.0 0.7 fusion.1
  0.7 0.0 copy-done
  0.7 0.7 gather_fusion
  1.4 0.1 select_reduce_fusion.inv_ref
  1.5 0.0 copy-start.1
  1.6 1.2 %copy-done.1 = bf16[1,1,32,128,128]{4,3,2,1,0:T(8,128)(2,1)S(1)} copy-done((bf16[1,1,32,128,128]{4,3,2,1,0:T(8,128)(2,1)S(1)}, bf16[1,1,32,128,128]{4,3,2,1,0:T(8,128)(2,1)}, u32[]{:S(2)}) %copy-start.1) | copy-done | bytes 1048600
  2.8 99.4 %shard_map.37 = f32[32,128,128]{2,1,0:T(8,128)S(1)} custom-call(s32[32]{0:T(128)S(1)} %compare_select_fusion.1.jc_ref, s32[32]{0:T(128)S(1)} %select_reduce_fusion.inv_ref, bf16[32,128,128]{2,1,0:T(8,128)(2,1)S(1)} %bitcast.7), custom_call_target="tpu_custom_call" | custom-call | tf_op jit(solution)/shard_map/pallas_call | solution.py:266
  102.2 1.3 %copy.5 = f32[1,1,32,128,128]{4,3,2,1,0:T(8,128)} copy(f32[1,1,32,128,128]{4,3,2,1,0:T(8,128)S(1)} %bitcast.6) | data formatting | bytes 4194304
  (2 shorter events, 0.0 us)
Async XLA Ops:
  0.0 0.7 copy-start
  1.5 1.2 %copy-start.1 = (bf16[1,1,32,128,128]{4,3,2,1,0:T(8,128)(2,1)S(1)}, bf16[1,1,32,128,128]{4,3,2,1,0:T(8,128)(2,1)}, u32[]{:S(2)}) copy-start(bf16[1,1,32,128,128]{4,3,2,1,0:T(8,128)(2,1)} %param.4) | copy-start | bytes 3145732
